TPU v7x, 32 devices: a whole 2x2x4 slice. The times are simulated.
32 devices in a mesh: row: 4 (over y, x), col: 8 (over z, core).
Axes of the slice: x: 2, y: 2, z: 4, core: 2. Of those that a mesh axis runs over, the one named last changes fastest.
Arguments:
- points: float32 [8192, 64], P(('row', 'col')), may hold values from -6 to 6
- feature_scales: float32 [64], replicated, may hold values from 0.06 to 0.25
- amplitude: float32 [1], replicated, may hold values from 1 to 3
- ridge: float32 [1], replicated, may hold values from 0.5 to 2
Outputs:
- factored: float32 [12, 8, 16, 4, 2048], P(None, 'col', None, 'row')
All inputs are finite; a program needn't handle non-finite values.
Results may differ from a plain program's by a relative error of at most 0.0009.
The roundings to bfloat16 on the way count: a program that leaves them out, or rounds other values in their place, can miss the bound.
Values may be sent and summed in bfloat16 or wider, within the bound.
A program may use at most 128 MiB of HBM per device.

v0:
```python
import functools

import jax
import jax.numpy as jnp
from jax import lax
from jax.experimental import pallas as pl
from jax.experimental.pallas import tpu as pltpu
from jax.sharding import PartitionSpec as P

FEAT = 64
SLAB = 1536
PANEL = 256
BLK = 16
BASE = 64
SUB = 8
HIGHEST = lax.Precision.HIGHEST
MESH = pl.DeviceIdType.MESH


def pack(rows):
    half = rows.shape[-2] // 2
    return jnp.concatenate([rows[..., :half, :], rows[..., half:, :]], axis=-1)


def unpack(rows):
    return jnp.concatenate([rows[..., :FEAT], rows[..., FEAT:]], axis=-2)


def exchange_kernel(
    n_row, n_col, n_panel, n_trail,
    blocks, strips, rows_out, panel_out, trail_out,
    send_sem, recv_sem, trail_send, trail_recv, panel_send, panel_recv, local_sem,
):
    n_dev = n_row * n_col
    my_row = lax.axis_index("row")
    my_col = lax.axis_index("col")
    me = my_row * n_col + my_col
    has_trail = jnp.logical_and(me >= n_panel, me < n_panel + n_trail)

    def place(step):
        peer = lax.rem(me + step, n_dev)
        return peer, lax.div(peer, n_col), lax.rem(peer, n_col)

    barrier = pltpu.get_barrier_semaphore()

    @pl.loop(1, n_dev)
    def _(step):
        _, row, col = place(step)
        pl.semaphore_signal(barrier, inc=1, device_id=(row, col), device_id_type=MESH)

    pl.semaphore_wait(barrier, n_dev - 1)

    def block_copy(step):
        _, row, col = place(step)
        return pltpu.make_async_remote_copy(
            src_ref=blocks.at[row], dst_ref=rows_out.at[me],
            send_sem=send_sem.at[step], recv_sem=recv_sem.at[me],
            device_id=(row, col), device_id_type=MESH,
        )

    def trail_copy(step):
        _, row, col = place(step)
        return pltpu.make_async_remote_copy(
            src_ref=strips.at[:, col], dst_ref=trail_out.at[me - n_panel],
            send_sem=trail_send.at[step], recv_sem=trail_recv.at[me - n_panel],
            device_id=(row, col), device_id_type=MESH,
        )

    def panel_copy(source, step):
        row = lax.rem(my_row + step, n_row)
        return pltpu.make_async_remote_copy(
            src_ref=rows_out.at[source], dst_ref=panel_out.at[source, my_row],
            send_sem=panel_send.at[source, step], recv_sem=panel_recv.at[source, my_row],
            device_id=(row, my_col), device_id_type=MESH,
        )

    def arrival(source):
        return pltpu.make_async_remote_copy(
            src_ref=blocks.at[0], dst_ref=rows_out.at[source],
            send_sem=send_sem.at[0], recv_sem=recv_sem.at[source],
            device_id=(my_row, my_col), device_id_type=MESH,
        )

    @pl.loop(1, n_dev)
    def _(step):
        block_copy(step).start()

    own = pltpu.make_async_copy(blocks.at[my_row], rows_out.at[me], local_sem.at[0])
    own.start()
    own.wait()

    @pl.when(has_trail)
    def _():
        @pl.loop(1, n_dev)
        def _(step):
            trail_copy(step).start()

        kept = pltpu.make_async_copy(
            strips.at[:, my_col], trail_out.at[me - n_panel], local_sem.at[0]
        )
        kept.start()
        kept.wait()

    for source in range(n_panel):
        @pl.when(me != source)
        def _():
            arrival(source).wait_recv()

        kept = pltpu.make_async_copy(
            rows_out.at[source], panel_out.at[source, my_row], local_sem.at[0]
        )
        kept.start()
        for step in range(1, n_row):
            panel_copy(source, step).start()
        kept.wait()

    @pl.loop(n_panel, n_dev)
    def _(source):
        @pl.when(me != source)
        def _():
            arrival(source).wait_recv()

    @pl.loop(0, n_trail)
    def _(source):
        @pl.when(me != source + n_panel)
        def _():
            pltpu.make_async_remote_copy(
                src_ref=strips.at[:, my_col], dst_ref=trail_out.at[source],
                send_sem=trail_send.at[0], recv_sem=trail_recv.at[source],
                device_id=(my_row, my_col), device_id_type=MESH,
            ).wait_recv()

    for source in range(n_panel):
        for step in range(1, n_row):
            row = lax.rem(my_row + step, n_row)
            pltpu.make_async_remote_copy(
                src_ref=rows_out.at[source], dst_ref=panel_out.at[source, row],
                send_sem=panel_send.at[source, 0], recv_sem=panel_recv.at[source, row],
                device_id=(my_row, my_col), device_id_type=MESH,
            ).wait_recv()
            panel_copy(source, step).wait_send()

    @pl.loop(1, n_dev)
    def _(step):
        block_copy(step).wait_send()

    @pl.when(has_trail)
    def _():
        @pl.loop(1, n_dev)
        def _(step):
            trail_copy(step).wait_send()


def exchange(points, n_row, n_col):
    rows_one = points.shape[0]
    n_dev = n_row * n_col
    block_rows = rows_one // n_row
    n_panel = 2 * PANEL // rows_one
    n_trail = SLAB // rows_one - n_panel
    strips_one = rows_one // (BLK * n_col)
    blocks = pack(points.reshape(n_row, block_rows, FEAT))
    strips = pack(points.reshape(strips_one, n_col, BLK, FEAT))
    piece = (block_rows // 2, 2 * FEAT)
    vmem = pl.BlockSpec(memory_space=pltpu.VMEM)
    rows, panel, trail = pl.pallas_call(
        functools.partial(exchange_kernel, n_row, n_col, n_panel, n_trail),
        out_shape=(
            jax.ShapeDtypeStruct((n_dev, *piece), jnp.float32),
            jax.ShapeDtypeStruct((n_panel, n_row, *piece), jnp.float32),
            jax.ShapeDtypeStruct((n_trail, strips_one, BLK // 2, 2 * FEAT), jnp.float32),
        ),
        in_specs=[vmem] * 2,
        out_specs=(vmem,) * 3,
        scratch_shapes=[
            pltpu.SemaphoreType.DMA((n_dev,)),
            pltpu.SemaphoreType.DMA((n_dev,)),
            pltpu.SemaphoreType.DMA((n_dev,)),
            pltpu.SemaphoreType.DMA((n_trail,)),
            pltpu.SemaphoreType.DMA((n_panel, n_row)),
            pltpu.SemaphoreType.DMA((n_panel, n_row)),
            pltpu.SemaphoreType.DMA((1,)),
        ],
        compiler_params=pltpu.CompilerParams(collective_id=0, has_side_effects=True),
    )(blocks, strips)
    return (
        unpack(rows).reshape(-1, FEAT),
        unpack(panel).reshape(-1, FEAT),
        unpack(trail).reshape(-1, FEAT),
    )


def base_inverse(block):
    row = lax.broadcasted_iota(jnp.int32, (BASE, BASE), 0)
    col = lax.broadcasted_iota(jnp.int32, (BASE, BASE), 1)
    both = jnp.concatenate([block, (row == col).astype(jnp.float32)], axis=1)
    groups = BASE // SUB
    full = (SUB, 2 * BASE)
    rows = [both[SUB * g : SUB * (g + 1)] for g in range(groups)]
    inside = lax.broadcasted_iota(jnp.int32, full, 0)
    for g in range(groups):
        cols = [
            {b: jnp.broadcast_to(rows[b][:, SUB * g + j : SUB * g + j + 1], full) for b in range(g, groups)}
            for j in range(SUB)
        ]
        scale = jnp.zeros(full, jnp.float32)
        for j in range(SUB):
            own = cols[j][g]
            pivot = jnp.broadcast_to(own[j : j + 1], full)
            inverse = 1.0 / pivot
            scale = jnp.where(inside == j, lax.rsqrt(pivot), scale)
            lead = jnp.broadcast_to(rows[g][j : j + 1], full) * inverse
            factors = dict(cols[j])
            factors[g] = jnp.where(inside > j, own, 0.0)
            for k in range(j + 1, SUB):
                weight = jnp.broadcast_to(own[k : k + 1], full) * inverse
                for b in range(g, groups):
                    cols[k][b] = cols[k][b] - factors[b] * weight
            for b in range(g, groups):
                rows[b] = rows[b] - factors[b] * lead
        rows[g] = rows[g] * scale
    return jnp.concatenate([r[:, BASE:] for r in rows], axis=0)


def full_dot(a, b, dims=((1,), (0,))):
    return lax.dot_general(
        a, b, (dims, ((), ())), precision=HIGHEST, preferred_element_type=jnp.float32
    )


def inverse_factor(a, out_ref, work):
    work[:, :PANEL] = (a + a.T) * 0.5
    row = lax.broadcasted_iota(jnp.int32, (PANEL, PANEL), 0)
    col = lax.broadcasted_iota(jnp.int32, (PANEL, PANEL), 1)
    work[:, PANEL:] = (row == col).astype(jnp.float32)
    lane = lax.broadcasted_iota(jnp.int32, (BASE, PANEL), 1)

    @pl.loop(0, PANEL // BASE)
    def _(step):
        start = pl.multiple_of(step * BASE, BASE)
        strip = work[pl.ds(start, BASE), :]
        turned = pltpu.roll(strip[:, :PANEL], lax.rem(PANEL - start, PANEL), 1)
        inverse = base_inverse(turned[:, :BASE])
        solved = full_dot(inverse, strip)
        below = jnp.where(lane >= start + BASE, solved[:, :PANEL], 0.0)
        work[...] = work[...] - full_dot(below, solved, ((0,), (0,)))
        out_ref[pl.ds(start, BASE), :] = solved[:, PANEL:]


def inverse_kernel(a_ref, out_ref, work):
    inverse_factor(a_ref[...], out_ref, work)


def lower_inverse(block):
    return pl.pallas_call(
        inverse_kernel,
        out_shape=jax.ShapeDtypeStruct((PANEL, PANEL), jnp.float32),
        in_specs=[pl.BlockSpec(memory_space=pltpu.VMEM)],
        out_specs=pl.BlockSpec(memory_space=pltpu.VMEM),
        scratch_shapes=[pltpu.VMEM((PANEL, 2 * PANEL), jnp.float32)],
        compiler_params=pltpu.CompilerParams(vmem_limit_bytes=32 * 1024 * 1024),
    )(block)


def kernel_rows(left, right, scales, signal):
    left_scaled = left * scales
    right_scaled = right * scales
    left_norms = jnp.sum(left_scaled * left_scaled, axis=1)
    right_norms = jnp.sum(right_scaled * right_scaled, axis=1)
    cross = jnp.dot(
        left_scaled, right_scaled.T, precision=HIGHEST, preferred_element_type=jnp.float32
    )
    return signal * jnp.exp(-0.5 * (left_norms[:, None] + right_norms[None, :] - 2.0 * cross))


def on_device(points, feature_scales, amplitude, ridge):
    n_row = lax.axis_size("row")
    n_col = lax.axis_size("col")
    block_rows = points.shape[0] // n_row
    n_points = points.shape[0] * n_col
    col_blocks = SLAB // (BLK * n_col)
    panel_blocks = PANEL // (BLK * n_col)
    signal = amplitude[0]
    jitter = ridge[0]
    process_row = lax.axis_index("row")
    column = lax.axis_index("col")
    row_points, panel_centers, own_centers = exchange(points, n_row, n_col)
    chosen = jnp.concatenate([panel_centers, own_centers], axis=0)

    center = kernel_rows(chosen, panel_centers, feature_scales, signal)
    center = center + jitter * jnp.eye(chosen.shape[0], 2 * PANEL, dtype=jnp.float32)
    first_inverse = lower_inverse(center[:PANEL, :PANEL])
    center_first = jnp.dot(
        center[PANEL:, :PANEL], first_inverse.T, precision=HIGHEST, preferred_element_type=jnp.float32
    ).astype(jnp.bfloat16)
    center_second = center[PANEL:, PANEL:] - jnp.dot(
        center_first, center_first[:PANEL].T, preferred_element_type=jnp.float32
    )
    second_inverse = lower_inverse(center_second[:PANEL])
    second_part = jnp.dot(
        center_second[PANEL:], second_inverse.T, precision=HIGHEST, preferred_element_type=jnp.float32
    ).astype(jnp.bfloat16)
    own_table = jnp.concatenate([center_first[PANEL:], second_part], axis=1)

    kernel = kernel_rows(chosen, row_points, feature_scales, signal)
    shape = kernel.shape
    trail = col_blocks - 2 * panel_blocks
    owned = (
        (lax.broadcasted_iota(jnp.int32, (trail, BLK), 0) + 2 * panel_blocks) * n_col + column
    ) * BLK + lax.broadcasted_iota(jnp.int32, (trail, BLK), 1)
    col_index = jnp.concatenate(
        [lax.broadcasted_iota(jnp.int32, (2 * PANEL,), 0), owned.reshape(-1)]
    )[:, None]
    grid_pos = lax.broadcasted_iota(jnp.int32, shape, 1)
    row_index = (grid_pos // block_rows * n_row + process_row) * block_rows + grid_pos % block_rows
    kernel = kernel + jnp.where(col_index == row_index, jitter, jnp.float32(0.0))
    first_panel = jnp.dot(
        first_inverse, kernel[:PANEL], precision=HIGHEST, preferred_element_type=jnp.float32
    ).astype(jnp.bfloat16)
    adjusted = kernel[PANEL : 2 * PANEL] - jnp.dot(
        center_first[:PANEL], first_panel, preferred_element_type=jnp.float32
    )
    second_panel = jnp.dot(
        second_inverse, adjusted, precision=HIGHEST, preferred_element_type=jnp.float32
    ).astype(jnp.bfloat16)
    both_panels = jnp.concatenate([first_panel, second_panel], axis=0)
    trailing = kernel[2 * PANEL :] - jnp.dot(
        own_table, both_panels, preferred_element_type=jnp.float32
    )
    own_panels = lax.dynamic_index_in_dim(
        both_panels.reshape(2 * panel_blocks, n_col, BLK, n_points), column, 1, False
    ).astype(jnp.float32)
    finished = jnp.concatenate([own_panels, trailing.reshape(trail, BLK, n_points)], axis=0)
    return finished.reshape(col_blocks, 1, BLK, 1, n_points)


def solution(mesh):
    placed = (P(("row", "col"), None), P(), P(), P())
    return jax.shard_map(
        on_device,
        mesh=mesh,
        in_specs=placed,
        out_specs=P(None, "col", None, "row", None),
        check_vma=False,
    )
```

profile of v0, /device:TPU:0, one launch (start us, length us, event | category | flops | bytes accessed | tf_op | source)
XLA Modules:
  0.0 72.1 jit_solution(16839698564100246906)
XLA Ops:
  0.0 0.0 copy-start.2
  1.3 0.1 iota_add_fusion
  1.4 0.1 add.95
  1.5 0.9 %copy.5 = f32[256,64]{1,0:T(8,128)S(1)} copy(f32[256,64]{0,1:T(8,128)} %param.4) | data formatting | bytes 131072 | tf_op args[0]
  2.5 0.7 pad_maximum_fusion.4.blocks
  3.2 0.7 pad_maximum_fusion.5.strips
  3.9 25.1 %shard_map.46 = (f32[32,32,128]{2,1,0:T(8,128)}, f32[2,4,32,128]{3,2,1,0:T(8,128)}, f32[4,2,8,128]{3,2,1,0:T(8,128)}) custom-call(f32[4,32,128]{2,1,0:T(8,128)} %pad_maximum_fusion.4.blocks, f32[2,8,8,128]{3,2,1,0:T(8,128)} %pad_maximum_fusion.5.strips), custom_call_target="tpu_custom_call" | custom-call | tf_op jit(solution)/shard_map/pallas_call | solution.py:165
  29.0 0.0 copy-start.1
  29.0 0.9 %fusion.30 = (f32[4,2,8,64]{3,2,1,0:T(8,128)S(1)}, f32[4,2,8,64]{3,2,1,0:T(8,128)S(1)}) fusion(f32[4,2,8,128]{3,2,1,0:T(8,128)} %get-tuple-element.9), kind=kLoop, calls=%fused_computation.61 | loop fusion | bytes 65536 | tf_op jit(solution)/shard_map/slice | solution.py:26
  29.9 1.1 %fusion.27 = (f32[2,4,32,64]{3,2,1,0:T(8,128)S(1)}, f32[2,4,32,64]{3,2,1,0:T(8,128)S(1)}) fusion(f32[2,4,32,128]{3,2,1,0:T(8,128)} %get-tuple-element.8), kind=kLoop, calls=%fused_computation.58 | loop fusion | bytes 262144 | tf_op jit(solution)/shard_map/slice | solution.py:26
  31.0 0.0 copy-done.2
  31.0 0.2 multiply_reduce_fusion.2
  31.2 0.1 add.82
  31.3 0.2 multiply_reduce_fusion.1
  31.4 0.0 copy-done.1
  31.4 0.2 fusion.26
  31.7 0.4 multiply_reduce_fusion
  32.0 0.1 add.87
  32.1 0.1 bitcast_multiply_fusion
  32.2 1.5 %fusion.5 = f32[640,512]{1,0:T(8,128)S(1)} fusion(f32[]{:T(128)} %bitcast.25, f32[512]{0:T(512)S(1)} %add.82, f32[640]{0:T(1024)S(1)} %multiply_reduce_fusion.1, f32[]{:T(128)} %bitcast.23, f32[512,64]{1,0:T(8,128)S(1)} %bitcast.32, f32[128,64]{1,0:T(8,128)S(1)} %bitcast.35, f32[64]{0:T(128)S(1)} %copy-done.2), kind=kOutput, calls=%fused_computation.14 | convolution fusion | flops 254394368 | bytes 1479432 | tf_op jit(solution)/shard_map/dot_general | solution.py:269
  33.7 11.8 %shard_map.47 = f32[256,256]{1,0:T(8,128)S(1)} custom-call(f32[256,256]{1,0:T(8,128)S(1)} %slice.85.a_ref), custom_call_target="tpu_custom_call" | custom-call | tf_op jit(solution)/shard_map/pallas_call | solution.py:254
  45.5 0.6 convolution_convert_fusion.2
  46.1 0.0 copy-start
  46.1 0.3 convolution_subtract_fusion.2
  46.4 12.0 %shard_map.48 = f32[256,256]{1,0:T(8,128)S(1)} custom-call(f32[256,256]{1,0:T(8,128)S(1)} %slice.90.a_ref), custom_call_target="tpu_custom_call" | custom-call | tf_op jit(solution)/shard_map/pallas_call | solution.py:254
  58.3 0.4 convolution_convert_fusion.3
  58.7 5.9 %select_add_fusion = f32[640,2048]{1,0:T(8,128)S(1)} fusion(f32[2048,64]{1,0:T(8,128)S(1)} %bitcast_multiply_fusion, f32[]{:T(128)} %bitcast.26, s32[2048]{0:T(1024)S(1)} %get-tuple-element.26, s32[2048]{0:T(1024)S(1)} %get-tuple-element.27, s32[]{:T(128)S(6)} %axis_index.25, s32[2048]{0:T(1024)S(1)} %get-tuple-element.25, s32[2048]{0:T(1024)S(1)} %get-tuple-element.28, ...), kind=kOutput, calls=%fused_computation | convolution fusion | flops 1025064960 | bytes 5981452 | tf_op jit(solution)/shard_map/dot_general | solution.py:269
  64.6 1.9 %convolution_convert_fusion.1 = bf16[256,2048]{1,0:T(8,128)(2,1)S(1)} fusion(f32[256,256]{1,0:T(8,128)S(1)} %shard_map.47, f32[640,2048]{1,0:T(8,128)S(1)} %select_add_fusion), kind=kOutput, calls=%fused_computation.4 | convolution fusion | flops 1611137024 | bytes 3407872 | tf_op jit(solution)/shard_map/dot_general | solution.py:316
  66.6 0.0 copy-done
  66.6 0.5 convolution_subtract_fusion
  67.0 0.0 slice-start
  67.1 1.9 %convolution_convert_fusion = bf16[256,2048]{1,0:T(8,128)(2,1)S(1)} fusion(f32[256,256]{1,0:T(8,128)S(1)} %shard_map.48, f32[256,2048]{1,0:T(8,128)S(1)} %convolution_subtract_fusion), kind=kOutput, calls=%fused_computation.3 | convolution fusion | flops 1611137024 | bytes 3407872 | tf_op jit(solution)/shard_map/dot_general | solution.py:322
  69.0 0.0 slice-done
  69.0 0.5 convolution_subtract_fusion.1
  69.5 0.2 pad_maximum_fusion
  69.8 0.1 pad_maximum_fusion.1
  69.9 2.2 %reshape.60 = f32[12,1,16,1,2048]{4,3,2,1,0:T(1,128)} reshape(f32[12,16,2048]{2,1,0:T(8,128)S(1)} %pad_maximum_fusion.1) | data formatting | bytes 3145728 | tf_op jit(solution)/shard_map/reshape | solution.py:333
  (12 shorter events, 0.1 us)
Async XLA Ops:
  0.0 31.0 %copy-start.2 = (f32[64]{0:T(128)S(1)}, f32[64]{0:T(128)}, u32[]{:S(2)}) copy-start(f32[64]{0:T(128)} %param.5) | copy-start | bytes 772
  29.0 2.4 %copy-start.1 = (f32[32,32,128]{2,1,0:T(8,128)S(1)}, f32[32,32,128]{2,1,0:T(8,128)}, u32[]{:S(2)}) copy-start(f32[32,32,128]{2,1,0:T(8,128)} %get-tuple-element.10) | copy-start | bytes 1572868
  46.1 20.5 %copy-start = (bf16[384,256]{0,1:T(8,128)(2,1)}, bf16[384,256]{0,1:T(8,128)(2,1)S(1)}, u32[]{:S(2)}) copy-start(bf16[384,256]{0,1:T(8,128)(2,1)S(1)} %convolution_convert_fusion.2) | copy-start | bytes 589828
  67.0 1.9 %slice-start = ((bf16[384,256]{0,1:T(8,128)(2,1)}), bf16[128,256]{0,1:T(8,128)(2,1)S(1)}, s32[]{:S(2)}) async-start(bf16[384,256]{0,1:T(8,128)(2,1)} %copy-done), calls=%async_computation | async-start | bytes 131072 | tf_op jit(solution)/shard_map/slice | solution.py:302
where the time goes:
time: 72.4 us; the launch traced here: 72.1 us
  Pallas kernels  48.8 us (67%)
  matrix products  13.4 us (19%)
  local copies, waits for them, and re-layouts  5.69 us (8%)
  other arithmetic  2.68 us (4%)
  between operations  1.57 us (2%)
    pallas_call x1, Pallas kernels, exchange(): pl.pallas_call(functools.partial(exchange_kernel, n_row, n_col, n_panel,...  25.1 us
    pallas_call x2, Pallas kernels, lower_inverse(): pl.pallas_call(inverse_kernel, out_shape=jax.ShapeDtypeStruct((PANEL, PAN...  23.7 us
    dot_general x2, matrix products, kernel_rows(): jnp.dot(left_scaled, right_scaled.T, precision=HIGHEST, preferred_element...  7.4 us
    reshape x1, local copies, waits for them, and re-layouts, on_device(): return finished.reshape(col_blocks, 1, BLK, 1, n_points)  2.25 us
    slice x3, local copies, waits for them, and re-layouts, unpack(): return jnp.concatenate([rows[..., :FEAT], rows[..., FEAT:]], axis=-2)  2.19 us
    dot_general x1, matrix products, on_device(): jnp.dot(second_inverse, adjusted, precision=HIGHEST, preferred_element_ty...  1.92 us
    dot_general x1, matrix products, on_device(): jnp.dot(first_inverse, kernel[:PANEL], precision=HIGHEST, preferred_eleme...  1.91 us

commit v1 on v0

v1 whole, which is shorter than its diff:
```python
import functools

import jax
import jax.numpy as jnp
from jax import lax
from jax.experimental import pallas as pl
from jax.experimental.pallas import tpu as pltpu
from jax.sharding import PartitionSpec as P

FEAT = 64
SLAB = 1536
PANEL = 256
BLK = 16
BASE = 64
SUB = 8
HIGHEST = lax.Precision.HIGHEST
MESH = pl.DeviceIdType.MESH


def pack(rows):
    half = rows.shape[-2] // 2
    return jnp.concatenate([rows[..., :half, :], rows[..., half:, :]], axis=-1)


def unpack(rows):
    return jnp.concatenate([rows[..., :FEAT], rows[..., FEAT:]], axis=-2)


def split(x):
    high = x.astype(jnp.bfloat16)
    rest = x - high.astype(jnp.float32)
    middle = rest.astype(jnp.bfloat16)
    low = (rest - middle.astype(jnp.float32)).astype(jnp.bfloat16)
    return high, middle, low


def joined_dot(a, b, dims):
    ah, am, al = split(a)
    bh, bm, bl = split(b)
    left = jnp.concatenate([ah, ah, am, ah, al, am], axis=dims[0][0])
    right = jnp.concatenate([bh, bm, bh, bl, bh, bm], axis=dims[1][0])
    return lax.dot_general(left, right, (dims, ((), ())), preferred_element_type=jnp.float32)


def gaussian(left, right, signal):
    left_norms = 0.5 * jnp.sum(left * left, axis=1, keepdims=True)
    right_norms = full_dot(jnp.full((8, FEAT), 0.5, jnp.float32), right * right, ((1,), (1,)))[:1]
    cross = joined_dot(left, right, ((1,), (1,)))
    return signal * jnp.exp(cross - left_norms - right_norms)


def factor_kernel(
    n_row, n_col, n_panel, n_trail,
    numbers, points, scales,
    rows_out, panel_out, trail_out, inverse_one, inverse_two, second_rows, own_table,
    blocks, strips, work_a, work_x,
    send_sem, recv_sem, trail_send, trail_recv, panel_send, panel_recv, local_sem,
):
    n_dev = n_row * n_col
    my_row = lax.axis_index("row")
    my_col = lax.axis_index("col")
    me = my_row * n_col + my_col
    has_trail = jnp.logical_and(me >= n_panel, me < n_panel + n_trail)
    has_panel = me < n_panel
    values = points[...]
    blocks[...] = pack(values.reshape(blocks.shape[0], -1, FEAT))
    strips[...] = pack(values.reshape(strips.shape[0], strips.shape[1], BLK, FEAT))

    def place(step):
        peer = lax.rem(me + step, n_dev)
        return peer, lax.div(peer, n_col), lax.rem(peer, n_col)

    barrier = pltpu.get_barrier_semaphore()

    @pl.loop(1, n_dev)
    def _(step):
        _, row, col = place(step)
        pl.semaphore_signal(barrier, inc=1, device_id=(row, col), device_id_type=MESH)

    pl.semaphore_wait(barrier, n_dev - 1)

    def block_copy(step):
        _, row, col = place(step)
        return pltpu.make_async_remote_copy(
            src_ref=blocks.at[row], dst_ref=rows_out.at[me],
            send_sem=send_sem.at[step], recv_sem=recv_sem.at[me],
            device_id=(row, col), device_id_type=MESH,
        )

    def trail_copy(step):
        _, row, col = place(step)
        return pltpu.make_async_remote_copy(
            src_ref=strips.at[:, col], dst_ref=trail_out.at[me - n_panel],
            send_sem=trail_send.at[step], recv_sem=trail_recv.at[me - n_panel],
            device_id=(row, col), device_id_type=MESH,
        )

    def panel_copy(source, step):
        row = lax.rem(my_row + step, n_row)
        return pltpu.make_async_remote_copy(
            src_ref=rows_out.at[source], dst_ref=panel_out.at[source, my_row],
            send_sem=panel_send.at[source, step], recv_sem=panel_recv.at[source, my_row],
            device_id=(row, my_col), device_id_type=MESH,
        )

    def arrival(source):
        return pltpu.make_async_remote_copy(
            src_ref=blocks.at[0], dst_ref=rows_out.at[source],
            send_sem=send_sem.at[0], recv_sem=recv_sem.at[source],
            device_id=(my_row, my_col), device_id_type=MESH,
        )

    def send_blocks():
        @pl.loop(1, n_dev)
        def _(step):
            block_copy(step).start()

    pl.when(has_panel)(send_blocks)

    own = pltpu.make_async_copy(blocks.at[my_row], rows_out.at[me], local_sem.at[0])
    own.start()
    own.wait()

    for source in range(n_panel):
        @pl.when(me != source)
        def _():
            arrival(source).wait_recv()

        kept = pltpu.make_async_copy(
            rows_out.at[source], panel_out.at[source, my_row], local_sem.at[0]
        )
        kept.start()
        for step in range(1, n_row):
            panel_copy(source, step).start()
        kept.wait()

    @pl.when(has_trail)
    def _():
        @pl.loop(1, n_dev)
        def _(step):
            trail_copy(step).start()

        kept = pltpu.make_async_copy(
            strips.at[:, my_col], trail_out.at[me - n_panel], local_sem.at[0]
        )
        kept.start()
        kept.wait()

    pl.when(jnp.logical_not(has_panel))(send_blocks)

    for source in range(n_panel):
        for step in range(1, n_row):
            row = lax.rem(my_row + step, n_row)
            pltpu.make_async_remote_copy(
                src_ref=rows_out.at[source], dst_ref=panel_out.at[source, row],
                send_sem=panel_send.at[source, 0], recv_sem=panel_recv.at[source, row],
                device_id=(my_row, my_col), device_id_type=MESH,
            ).wait_recv()
            panel_copy(source, step).wait_send()

    signal = numbers[0]
    jitter = numbers[1]
    scale = scales[...]
    panel = unpack(panel_out[...]).reshape(2 * PANEL, FEAT) * scale
    center = gaussian(panel, panel, signal)
    row = lax.broadcasted_iota(jnp.int32, center.shape, 0)
    col = lax.broadcasted_iota(jnp.int32, center.shape, 1)
    center = center + jnp.where(row == col, jitter, 0.0)
    inverse_factor(center[:PANEL, :PANEL], inverse_one, work_a, work_x)
    low_first = full_dot(center[PANEL:, :PANEL], inverse_one[...], ((1,), (1,))).astype(jnp.bfloat16)
    second_rows[...] = low_first
    low_second = center[PANEL:, PANEL:] - plain_dot(low_first, low_first, ((1,), (1,)))
    inverse_factor(low_second, inverse_two, work_a, work_x)

    @pl.loop(0, n_trail)
    def _(source):
        @pl.when(me != source + n_panel)
        def _():
            pltpu.make_async_remote_copy(
                src_ref=strips.at[:, my_col], dst_ref=trail_out.at[source],
                send_sem=trail_send.at[0], recv_sem=trail_recv.at[source],
                device_id=(my_row, my_col), device_id_type=MESH,
            ).wait_recv()

    owned = unpack(trail_out[...]).reshape(-1, FEAT) * scale
    own = gaussian(owned, panel, signal)
    own_first = full_dot(own[:, :PANEL], inverse_one[...], ((1,), (1,))).astype(jnp.bfloat16)
    own_second = own[:, PANEL:] - plain_dot(own_first, low_first, ((1,), (1,)))
    own_table[:, :PANEL] = own_first
    own_table[:, PANEL:] = full_dot(own_second, inverse_two[...], ((1,), (1,))).astype(jnp.bfloat16)

    @pl.loop(n_panel, n_dev)
    def _(source):
        @pl.when(me != source)
        def _():
            arrival(source).wait_recv()

    @pl.loop(1, n_dev)
    def _(step):
        block_copy(step).wait_send()

    @pl.when(has_trail)
    def _():
        @pl.loop(1, n_dev)
        def _(step):
            trail_copy(step).wait_send()


def exchange_and_factor(numbers, points, scales, n_row, n_col):
    rows_one = points.shape[0]
    n_dev = n_row * n_col
    n_panel = 2 * PANEL // rows_one
    n_trail = SLAB // rows_one - n_panel
    strips_one = rows_one // (BLK * n_col)
    piece = (rows_one // n_row // 2, 2 * FEAT)
    strip = (BLK // 2, 2 * FEAT)
    n_own = n_trail * strips_one * BLK
    vmem = pl.BlockSpec(memory_space=pltpu.VMEM)
    shape = jax.ShapeDtypeStruct
    return pl.pallas_call(
        functools.partial(factor_kernel, n_row, n_col, n_panel, n_trail),
        out_shape=(
            shape((n_dev, *piece), jnp.float32),
            shape((n_panel, n_row, *piece), jnp.float32),
            shape((n_trail, strips_one, *strip), jnp.float32),
            shape((PANEL, PANEL), jnp.float32),
            shape((PANEL, PANEL), jnp.float32),
            shape((PANEL, PANEL), jnp.bfloat16),
            shape((n_own, 2 * PANEL), jnp.bfloat16),
        ),
        in_specs=[pl.BlockSpec(memory_space=pltpu.SMEM), vmem, vmem],
        out_specs=(vmem,) * 7,
        scratch_shapes=[
            pltpu.VMEM((n_row, *piece), jnp.float32),
            pltpu.VMEM((strips_one, n_col, *strip), jnp.float32),
            pltpu.VMEM((PANEL, PANEL), jnp.float32),
            pltpu.VMEM((PANEL, PANEL), jnp.float32),
            pltpu.SemaphoreType.DMA((n_dev,)),
            pltpu.SemaphoreType.DMA((n_dev,)),
            pltpu.SemaphoreType.DMA((n_dev,)),
            pltpu.SemaphoreType.DMA((n_trail,)),
            pltpu.SemaphoreType.DMA((n_panel, n_row)),
            pltpu.SemaphoreType.DMA((n_panel, n_row)),
            pltpu.SemaphoreType.DMA((1,)),
        ],
        compiler_params=pltpu.CompilerParams(
            collective_id=0, has_side_effects=True, vmem_limit_bytes=40 * 1024 * 1024
        ),
    )(numbers, points, scales)


def base_inverse(block):
    row = lax.broadcasted_iota(jnp.int32, (BASE, BASE), 0)
    col = lax.broadcasted_iota(jnp.int32, (BASE, BASE), 1)
    both = jnp.concatenate([block, (row == col).astype(jnp.float32)], axis=1)
    groups = BASE // SUB
    done = []
    for g in range(groups):
        height = BASE - SUB * g
        shape = (height, 2 * BASE)
        inside = lax.broadcasted_iota(jnp.int32, shape, 0)
        cols = [jnp.broadcast_to(both[:, SUB * g + j : SUB * g + j + 1], shape) for j in range(SUB)]
        scale = jnp.zeros((SUB, BASE), jnp.float32)
        for j in range(SUB):
            pivot = cols[j][j : j + 1]
            inverse = 1.0 / pivot
            scale = jnp.where(inside[:SUB, :BASE] == j, lax.rsqrt(pivot[:, :BASE]), scale)
            factors = jnp.where(inside > j, cols[j], 0.0)
            for k in range(j + 1, SUB):
                cols[k] = cols[k] - factors * (cols[j][k : k + 1] * inverse)
            both = both - factors * (both[j : j + 1] * inverse)
        done.append(both[:SUB, BASE:] * scale)
        both = both[SUB:]
    return jnp.concatenate(done, axis=0)


def full_dot(a, b, dims=((1,), (0,))):
    return lax.dot_general(
        a, b, (dims, ((), ())), precision=HIGHEST, preferred_element_type=jnp.float32
    )


def plain_dot(a, b, dims=((1,), (0,))):
    return lax.dot_general(a, b, (dims, ((), ())), preferred_element_type=jnp.float32)


def inverse_factor(a, out_ref, work_a, work_x):
    work_a[...] = (a + a.T) * 0.5
    row = lax.broadcasted_iota(jnp.int32, (PANEL, PANEL), 0)
    col = lax.broadcasted_iota(jnp.int32, (PANEL, PANEL), 1)
    work_x[...] = (row == col).astype(jnp.float32)
    out_ref[...] = jnp.zeros((PANEL, PANEL), jnp.float32)
    for start in range(0, PANEL, BASE):
        stop = start + BASE
        first = start // 128 * 128
        last = (stop + 127) // 128 * 128
        inverse = base_inverse(work_a[start:stop, start:stop])
        solved_x = joined_dot(inverse, work_x[start:stop, :last], ((1,), (0,)))
        out_ref[start:stop, :last] = solved_x
        if stop == PANEL:
            break
        solved_a = joined_dot(inverse, work_a[start:stop, first:], ((1,), (0,)))
        below = solved_a[:, stop - first :]
        kept = stop // 128 * 128
        work_a[stop:, kept:] -= joined_dot(below, solved_a[:, kept - first :], ((0,), (0,)))
        work_x[stop:, :last] -= joined_dot(below, solved_x, ((0,), (0,)))


def slab_kernel(
    n_row, n_col, block_rows,
    numbers, position, panel_ref, trail_ref, scales, one_ref, two_ref, second_ref, table_ref, rows_ref,
    out_ref, keep_one, keep_two, chosen_ref,
):
    signal = numbers[0]
    jitter = numbers[1]
    process_row = position[0]
    column = position[1]
    scale = scales[...]

    @pl.when(pl.program_id(0) == 0)
    def _():
        chosen_ref[: 2 * PANEL] = unpack(panel_ref[...]).reshape(2 * PANEL, FEAT) * scale
        chosen_ref[2 * PANEL :] = unpack(trail_ref[...]).reshape(-1, FEAT) * scale

    chunk = rows_ref.shape[0] * block_rows
    points = unpack(rows_ref[...]).reshape(chunk, FEAT) * scale
    kernel = gaussian(chosen_ref[...], points, signal)
    shape = kernel.shape
    group = BLK * n_col
    col = lax.broadcasted_iota(jnp.int32, (shape[0], 1), 0)
    extra = col - 2 * PANEL
    owned = 2 * PANEL + extra // BLK * group + column * BLK + extra % BLK
    col = jnp.where(extra >= 0, owned, col)
    place = pl.program_id(0) * chunk + lax.broadcasted_iota(jnp.int32, (1, chunk), 1)
    row = (place // block_rows * n_row + process_row) * block_rows + place % block_rows
    kernel = kernel + jnp.where(col == row, jitter, 0.0)
    first = full_dot(one_ref[...], kernel[:PANEL]).astype(jnp.bfloat16)
    reduced = kernel[PANEL : 2 * PANEL] - plain_dot(second_ref[...], first)
    second = full_dot(two_ref[...], reduced).astype(jnp.bfloat16)
    trailing = kernel[2 * PANEL :] - (
        plain_dot(table_ref[:, :PANEL], first) + plain_dot(table_ref[:, PANEL:], second)
    )
    keep_one[...] = first.astype(jnp.float32)
    keep_two[...] = second.astype(jnp.float32)
    blocks = PANEL // group
    for which, keep in enumerate((keep_one, keep_two)):
        for t in range(blocks):
            start = pl.multiple_of(t * group + column * BLK, BLK)
            at = (which * blocks + t) * BLK
            out_ref[at : at + BLK] = keep[pl.ds(start, BLK), :].reshape(BLK, 1, chunk)
    out_ref[2 * blocks * BLK :] = trailing.reshape(trailing.shape[0], 1, chunk)


def slab(numbers, position, factored, scales, n_row, n_col, block_rows):
    rows, panel, trail, one, two, second, table = factored
    n_dev = n_row * n_col
    together = 512 // block_rows
    chunk = together * block_rows
    n_own = table.shape[0]
    n_out = n_own + 2 * PANEL // n_col
    vmem = pl.BlockSpec(memory_space=pltpu.VMEM)
    smem = pl.BlockSpec(memory_space=pltpu.SMEM)
    return pl.pallas_call(
        functools.partial(slab_kernel, n_row, n_col, block_rows),
        grid=(n_dev // together,),
        out_shape=jax.ShapeDtypeStruct((n_out, 1, n_dev * block_rows), jnp.float32),
        in_specs=[smem, smem] + [vmem] * 7
        + [pl.BlockSpec((together, *rows.shape[1:]), lambda i: (i, 0, 0))],
        out_specs=pl.BlockSpec((n_out, 1, chunk), lambda i: (0, 0, i)),
        scratch_shapes=[
            pltpu.VMEM((PANEL, chunk), jnp.float32),
            pltpu.VMEM((PANEL, chunk), jnp.float32),
            pltpu.VMEM((2 * PANEL + n_own, FEAT), jnp.float32),
        ],
        compiler_params=pltpu.CompilerParams(vmem_limit_bytes=40 * 1024 * 1024),
    )(numbers, position, panel, trail, scales, one, two, second, table, rows)


def on_device(points, feature_scales, amplitude, ridge):
    n_row = lax.axis_size("row")
    n_col = lax.axis_size("col")
    block_rows = points.shape[0] // n_row
    numbers = jnp.concatenate([amplitude, ridge])
    position = jnp.stack([lax.axis_index("row"), lax.axis_index("col")]).astype(jnp.int32)
    scales = feature_scales[None]
    factored = exchange_and_factor(numbers, points, scales, n_row, n_col)
    finished = slab(numbers, position, factored, scales, n_row, n_col, block_rows)
    return finished.reshape(SLAB // (BLK * n_col), 1, BLK, 1, -1)


def solution(mesh):
    placed = (P(("row", "col"), None), P(), P(), P())
    return jax.shard_map(
        on_device,
        mesh=mesh,
        in_specs=placed,
        out_specs=P(None, "col", None, "row", None),
        check_vma=False,
    )
```

time: 72.4 us -> 57.9 us (0.80)
  the two profiles are of different devices: /device:TPU:0 before, /device:TPU:24 now
where the time goes in v1:
time: 57.9 us; the launch traced here: 57.8 us
  Pallas kernels  54.7 us (94%)
  local copies, waits for them, and re-layouts  1.58 us (3%)
  between operations  1.32 us (2%)
    pallas_call x1, Pallas kernels, exchange_and_factor(): pl.pallas_call(functools.partial(factor_kernel, n_row, n_col, n_panel, n_...  43.1 us
    pallas_call x1, Pallas kernels, slab(): pl.pallas_call(functools.partial(slab_kernel, n_row, n_col, block_rows),...  11.6 us
    unnamed x3, local copies, waits for them, and re-layouts  1.58 us

profile of v1, /device:TPU:24, one launch (start us, length us, event | category | flops | bytes accessed | tf_op | source)
XLA Modules:
  0.0 57.8 jit_solution(15711541922987536708)
XLA Ops:
  1.3 0.1 pad_maximum_fusion.numbers
  1.4 0.1 pad_add_fusion.position
  1.4 0.9 %copy.5.points = f32[256,64]{1,0:T(8,128)S(1)} copy(f32[256,64]{0,1:T(8,128)} %param.4) | data formatting | bytes 131072 | tf_op args[0]
  2.4 0.0 copy-start
  2.4 0.6 %copy-done = f32[64]{0:T(128)S(1)} copy-done((f32[64]{0:T(128)S(1)}, f32[64]{0:T(128)}, u32[]{:S(2)}) %copy-start) | copy-done | bytes 280
  3.0 43.1 %shard_map.46 = (f32[32,32,128]{2,1,0:T(8,128)S(1)}, f32[2,4,32,128]{3,2,1,0:T(8,128)S(1)}, f32[4,2,8,128]{3,2,1,0:T(8,128)S(1)}, f32[256,256]{1,0:T(8,128)S(1)}...) custom-call(f32[2]{0:T(128)S(1)} %pad_maximum_fusion.numbers, ...), custom_call_target="tpu_custom_call" | custom-call | tf_op jit(solution)/shard_map/pallas_call | solution.py:220
  46.2 11.6 %shard_map.47 = f32[192,1,2048]{2,1,0:T(1,128)} custom-call(f32[2]{0:T(128)S(1)} %pad_maximum_fusion.numbers, s32[2]{0:T(128)S(1)} %pad_add_fusion.position, f32[2,4,32,128]{3,2,1,0:T(8,128)S(1)} %get-tuple-element.12.panel_ref, f32[4,2,8,128]{3,2,1,0:T(8,128)S(1)} %get-tuple-element.13.trail_ref, f32[1,64]{1,0:T(1,128)S(1)} %bitcast.5, ...), custom_call_target="tpu_custom_call" | custom-call | tf_op jit(solution)/shard_map/pallas_call | solution.py:363
Async XLA Ops:
  2.4 0.7 %copy-start = (f32[64]{0:T(128)S(1)}, f32[64]{0:T(128)}, u32[]{:S(2)}) copy-start(f32[64]{0:T(128)} %param.5) | copy-start | bytes 772

commit v2 on v1

--- a/solution.py
+++ b/solution.py
@@ -52,8 +52,8 @@
 def factor_kernel(
     n_row, n_col, n_panel, n_trail,
     numbers, points, scales,
-    rows_out, panel_out, trail_out, inverse_one, inverse_two, second_rows, own_table,
-    blocks, strips, work_a, work_x,
+    rows_out, panel_out, trail_out, inverse_one, inverse_two, second_rows, own_table, scale_out,
+    turned, blocks, strips, work_a, work_x,
     send_sem, recv_sem, trail_send, trail_recv, panel_send, panel_recv, local_sem,
 ):
     n_dev = n_row * n_col
@@ -62,9 +62,6 @@
     me = my_row * n_col + my_col
     has_trail = jnp.logical_and(me >= n_panel, me < n_panel + n_trail)
     has_panel = me < n_panel
-    values = points[...]
-    blocks[...] = pack(values.reshape(blocks.shape[0], -1, FEAT))
-    strips[...] = pack(values.reshape(strips.shape[0], strips.shape[1], BLK, FEAT))
 
     def place(step):
         peer = lax.rem(me + step, n_dev)
@@ -77,6 +74,17 @@
         _, row, col = place(step)
         pl.semaphore_signal(barrier, inc=1, device_id=(row, col), device_id_type=MESH)
 
+    fetches = [
+        pltpu.make_async_copy(points, turned, local_sem.at[1]),
+        pltpu.make_async_copy(scales, scale_out, local_sem.at[2]),
+    ]
+    for fetch in fetches:
+        fetch.start()
+    for fetch in fetches:
+        fetch.wait()
+    values = turned[...].T
+    blocks[...] = pack(values.reshape(blocks.shape[0], -1, FEAT))
+    strips[...] = pack(values.reshape(strips.shape[0], strips.shape[1], BLK, FEAT))
     pl.semaphore_wait(barrier, n_dev - 1)
 
     def block_copy(step):
@@ -160,7 +168,7 @@
 
     signal = numbers[0]
     jitter = numbers[1]
-    scale = scales[...]
+    scale = scale_out[...]
     panel = unpack(panel_out[...]).reshape(2 * PANEL, FEAT) * scale
     center = gaussian(panel, panel, signal)
     row = lax.broadcasted_iota(jnp.int32, center.shape, 0)
@@ -216,6 +224,7 @@
     strip = (BLK // 2, 2 * FEAT)
     n_own = n_trail * strips_one * BLK
     vmem = pl.BlockSpec(memory_space=pltpu.VMEM)
+    whole = pl.BlockSpec(memory_space=pl.ANY)
     shape = jax.ShapeDtypeStruct
     return pl.pallas_call(
         functools.partial(factor_kernel, n_row, n_col, n_panel, n_trail),
@@ -227,10 +236,12 @@
             shape((PANEL, PANEL), jnp.float32),
             shape((PANEL, PANEL), jnp.bfloat16),
             shape((n_own, 2 * PANEL), jnp.bfloat16),
+            shape((1, FEAT), jnp.float32),
         ),
-        in_specs=[pl.BlockSpec(memory_space=pltpu.SMEM), vmem, vmem],
-        out_specs=(vmem,) * 7,
+        in_specs=[pl.BlockSpec(memory_space=pltpu.SMEM), whole, whole],
+        out_specs=(vmem,) * 8,
         scratch_shapes=[
+            pltpu.VMEM((FEAT, rows_one), jnp.float32),
             pltpu.VMEM((n_row, *piece), jnp.float32),
             pltpu.VMEM((strips_one, n_col, *strip), jnp.float32),
             pltpu.VMEM((PANEL, PANEL), jnp.float32),
@@ -241,12 +252,12 @@
             pltpu.SemaphoreType.DMA((n_trail,)),
             pltpu.SemaphoreType.DMA((n_panel, n_row)),
             pltpu.SemaphoreType.DMA((n_panel, n_row)),
-            pltpu.SemaphoreType.DMA((1,)),
+            pltpu.SemaphoreType.DMA((3,)),
         ],
         compiler_params=pltpu.CompilerParams(
             collective_id=0, has_side_effects=True, vmem_limit_bytes=40 * 1024 * 1024
         ),
-    )(numbers, points, scales)
+    )(numbers, points.T, scales)
 
 
 def base_inverse(block):
@@ -260,16 +271,31 @@
         shape = (height, 2 * BASE)
         inside = lax.broadcasted_iota(jnp.int32, shape, 0)
         cols = [jnp.broadcast_to(both[:, SUB * g + j : SUB * g + j + 1], shape) for j in range(SUB)]
-        scale = jnp.zeros((SUB, BASE), jnp.float32)
-        for j in range(SUB):
-            pivot = cols[j][j : j + 1]
-            inverse = 1.0 / pivot
-            scale = jnp.where(inside[:SUB, :BASE] == j, lax.rsqrt(pivot[:, :BASE]), scale)
-            factors = jnp.where(inside > j, cols[j], 0.0)
-            for k in range(j + 1, SUB):
-                cols[k] = cols[k] - factors * (cols[j][k : k + 1] * inverse)
-            both = both - factors * (both[j : j + 1] * inverse)
-        done.append(both[:SUB, BASE:] * scale)
+        pairs = []
+        for j in range(0, SUB, 2):
+            one, two = cols[j], cols[j + 1]
+            a, b, d = one[j : j + 1], one[j + 1 : j + 2], two[j + 1 : j + 2]
+            pairs.append((a, b, d))
+            inverse = pl.reciprocal(a * d - b * b)
+            first = jnp.where(inside > j + 1, one, 0.0)
+            second = jnp.where(inside > j + 1, two, 0.0)
+
+            def solved(u, v):
+                return (d * u - b * v) * inverse, (a * v - b * u) * inverse
+
+            for k in range(j + 2, SUB):
+                u, v = solved(one[k : k + 1], two[k : k + 1])
+                cols[k] = cols[k] - (first * u + second * v)
+            u, v = solved(both[j : j + 1], both[j + 1 : j + 2])
+            both = both - (first * u + second * v)
+        top = both[:SUB, BASE:]
+        lines = []
+        for j, (a, b, d) in zip(range(0, SUB, 2), pairs):
+            a, b, d = a[:, :BASE], b[:, :BASE], d[:, :BASE]
+            ratio = b / a
+            lines.append(top[j : j + 1] * lax.rsqrt(a))
+            lines.append((top[j + 1 : j + 2] - ratio * top[j : j + 1]) * lax.rsqrt(d - b * ratio))
+        done.append(jnp.concatenate(lines, axis=0))
         both = both[SUB:]
     return jnp.concatenate(done, axis=0)
 
@@ -351,8 +377,8 @@
     out_ref[2 * blocks * BLK :] = trailing.reshape(trailing.shape[0], 1, chunk)
 
 
-def slab(numbers, position, factored, scales, n_row, n_col, block_rows):
-    rows, panel, trail, one, two, second, table = factored
+def slab(numbers, position, factored, n_row, n_col, block_rows):
+    rows, panel, trail, one, two, second, table, scales = factored
     n_dev = n_row * n_col
     together = 512 // block_rows
     chunk = together * block_rows
@@ -384,7 +410,7 @@
     position = jnp.stack([lax.axis_index("row"), lax.axis_index("col")]).astype(jnp.int32)
     scales = feature_scales[None]
     factored = exchange_and_factor(numbers, points, scales, n_row, n_col)
-    finished = slab(numbers, position, factored, scales, n_row, n_col, block_rows)
+    finished = slab(numbers, position, factored, n_row, n_col, block_rows)
     return finished.reshape(SLAB // (BLK * n_col), 1, BLK, 1, -1)
 
 

time: 57.9 us -> 58.7 us (1.014)
  Pallas kernels: 54.7 us -> 55.6 us
    pallas_call x1, Pallas kernels: 43.1 us -> 44 us  [exchange_and_factor(): pl.pallas_call(functools.partial(factor_kernel, n_row, n_col, n_panel, n_...]
    unnamed x3 -> x4, local copies, waits for them, and re-layouts: 1.58 us -> 1.49 us
where the time goes in v2:
time: 58.7 us; the launch traced here: 58.6 us
  Pallas kernels  55.6 us (95%)
  local copies, waits for them, and re-layouts  1.49 us (3%)
  between operations  1.31 us (2%)
    pallas_call x1, Pallas kernels, exchange_and_factor(): pl.pallas_call(functools.partial(factor_kernel, n_row, n_col, n_panel, n_...  44 us
    pallas_call x1, Pallas kernels, slab(): pl.pallas_call(functools.partial(slab_kernel, n_row, n_col, block_rows),...  11.6 us
    unnamed x4, local copies, waits for them, and re-layouts  1.49 us

profile of v2, /device:TPU:24, one launch (start us, length us, event | category | flops | bytes accessed | tf_op | source)
XLA Modules:
  0.0 58.6 jit_solution(14543962158395742218)
XLA Ops:
  1.3 0.1 pad_maximum_fusion.numbers
  1.4 0.1 pad_add_fusion.position
  1.4 0.0 copy-start
  1.4 0.8 %copy-done = f32[256,64]{0,1:T(8,128)S(1)} copy-done((f32[256,64]{0,1:T(8,128)S(1)}, f32[256,64]{0,1:T(8,128)}, u32[]{:S(2)}) %copy-start) | copy-done | bytes 65560
  2.3 0.0 copy-start.1
  2.3 0.7 %copy-done.1 = f32[64]{0:T(128)S(1)} copy-done((f32[64]{0:T(128)S(1)}, f32[64]{0:T(128)}, u32[]{:S(2)}) %copy-start.1) | copy-done | bytes 280
  2.9 44.0 %shard_map.46 = (f32[32,32,128]{2,1,0:T(8,128)S(1)}, f32[2,4,32,128]{3,2,1,0:T(8,128)S(1)}, f32[4,2,8,128]{3,2,1,0:T(8,128)S(1)}, f32[256,256]{1,0:T(8,128)S(1)}...) custom-call(f32[2]{0:T(128)S(1)} %pad_maximum_fusion.numbers, ...), custom_call_target="tpu_custom_call" | custom-call | tf_op jit(solution)/shard_map/pallas_call | solution.py:229
  47.0 11.6 %shard_map.47 = f32[192,1,2048]{2,1,0:T(1,128)} custom-call(f32[2]{0:T(128)S(1)} %pad_maximum_fusion.numbers, s32[2]{0:T(128)S(1)} %pad_add_fusion.position, f32[2,4,32,128]{3,2,1,0:T(8,128)S(1)} %get-tuple-element.13.panel_ref, f32[4,2,8,128]{3,2,1,0:T(8,128)S(1)} %get-tuple-element.14.trail_ref, f32[1,64]{1,0:T(1,128)S(1)} %get-tuple-element.15.scales, ...), custom_call_target="tpu_custom_call" | custom-call | tf_op jit(solution)/shard_map/pallas_call | solution.py:389
Async XLA Ops:
  1.4 0.8 %copy-start = (f32[256,64]{0,1:T(8,128)S(1)}, f32[256,64]{0,1:T(8,128)}, u32[]{:S(2)}) copy-start(f32[256,64]{0,1:T(8,128)} %param.4) | copy-start | bytes 196612
  2.3 0.7 %copy-start.1 = (f32[64]{0:T(128)S(1)}, f32[64]{0:T(128)}, u32[]{:S(2)}) copy-start(f32[64]{0:T(128)} %param.5) | copy-start | bytes 772

commit v3 on v1

--- a/solution.py
+++ b/solution.py
@@ -167,11 +167,6 @@
     col = lax.broadcasted_iota(jnp.int32, center.shape, 1)
     center = center + jnp.where(row == col, jitter, 0.0)
     inverse_factor(center[:PANEL, :PANEL], inverse_one, work_a, work_x)
-    low_first = full_dot(center[PANEL:, :PANEL], inverse_one[...], ((1,), (1,))).astype(jnp.bfloat16)
-    second_rows[...] = low_first
-    low_second = center[PANEL:, PANEL:] - plain_dot(low_first, low_first, ((1,), (1,)))
-    inverse_factor(low_second, inverse_two, work_a, work_x)
-
     @pl.loop(0, n_trail)
     def _(source):
         @pl.when(me != source + n_panel)
@@ -182,11 +177,15 @@
                 device_id=(my_row, my_col), device_id_type=MESH,
             ).wait_recv()
 
+    low_first = full_dot(center[PANEL:, :PANEL], inverse_one[...], ((1,), (1,))).astype(jnp.bfloat16)
+    second_rows[...] = low_first
+    low_second = center[PANEL:, PANEL:] - plain_dot(low_first, low_first, ((1,), (1,)))
     owned = unpack(trail_out[...]).reshape(-1, FEAT) * scale
     own = gaussian(owned, panel, signal)
     own_first = full_dot(own[:, :PANEL], inverse_one[...], ((1,), (1,))).astype(jnp.bfloat16)
     own_second = own[:, PANEL:] - plain_dot(own_first, low_first, ((1,), (1,)))
     own_table[:, :PANEL] = own_first
+    inverse_factor(low_second, inverse_two, work_a, work_x)
     own_table[:, PANEL:] = full_dot(own_second, inverse_two[...], ((1,), (1,))).astype(jnp.bfloat16)
 
     @pl.loop(n_panel, n_dev)
@@ -300,10 +299,10 @@
         if stop == PANEL:
             break
         solved_a = joined_dot(inverse, work_a[start:stop, first:], ((1,), (0,)))
-        below = solved_a[:, stop - first :]
+        below = joined_dot(work_a[stop:, start:stop], inverse, ((1,), (1,)))
         kept = stop // 128 * 128
-        work_a[stop:, kept:] -= joined_dot(below, solved_a[:, kept - first :], ((0,), (0,)))
-        work_x[stop:, :last] -= joined_dot(below, solved_x, ((0,), (0,)))
+        work_a[stop:, kept:] -= joined_dot(below, solved_a[:, kept - first :], ((1,), (0,)))
+        work_x[stop:, :last] -= joined_dot(below, solved_x, ((1,), (0,)))
 
 
 def slab_kernel(

time: 57.9 us -> 56.8 us (0.981)
  Pallas kernels: 54.7 us -> 53.6 us
    pallas_call x1, Pallas kernels: 43.1 us -> 42 us  [exchange_and_factor(): pl.pallas_call(functools.partial(factor_kernel, n_row, n_col, n_panel, n_...]
where the time goes in v3:
time: 56.8 us; the launch traced here: 56.7 us
  Pallas kernels  53.6 us (94%)
  local copies, waits for them, and re-layouts  1.58 us (3%)
  between operations  1.32 us (2%)
    pallas_call x1, Pallas kernels, exchange_and_factor(): pl.pallas_call(functools.partial(factor_kernel, n_row, n_col, n_panel, n_...  42 us
    pallas_call x1, Pallas kernels, slab(): pl.pallas_call(functools.partial(slab_kernel, n_row, n_col, block_rows),...  11.6 us
    unnamed x3, local copies, waits for them, and re-layouts  1.58 us

profile of v3, /device:TPU:24, one launch (start us, length us, event | category | flops | bytes accessed | tf_op | source)
XLA Modules:
  0.0 56.7 jit_solution(14217130016040258723)
XLA Ops:
  1.3 0.1 pad_maximum_fusion.numbers
  1.4 0.1 pad_add_fusion.position
  1.4 0.9 %copy.5.points = f32[256,64]{1,0:T(8,128)S(1)} copy(f32[256,64]{0,1:T(8,128)} %param.4) | data formatting | bytes 131072 | tf_op args[0]
  2.4 0.0 copy-start
  2.4 0.6 %copy-done = f32[64]{0:T(128)S(1)} copy-done((f32[64]{0:T(128)S(1)}, f32[64]{0:T(128)}, u32[]{:S(2)}) %copy-start) | copy-done | bytes 280
  3.0 42.0 %shard_map.46 = (f32[32,32,128]{2,1,0:T(8,128)S(1)}, f32[2,4,32,128]{3,2,1,0:T(8,128)S(1)}, f32[4,2,8,128]{3,2,1,0:T(8,128)S(1)}, f32[256,256]{1,0:T(8,128)S(1)}...) custom-call(f32[2]{0:T(128)S(1)} %pad_maximum_fusion.numbers, ...), custom_call_target="tpu_custom_call" | custom-call | tf_op jit(solution)/shard_map/pallas_call | solution.py:219
  45.1 11.6 %shard_map.47 = f32[192,1,2048]{2,1,0:T(1,128)} custom-call(f32[2]{0:T(128)S(1)} %pad_maximum_fusion.numbers, s32[2]{0:T(128)S(1)} %pad_add_fusion.position, f32[2,4,32,128]{3,2,1,0:T(8,128)S(1)} %get-tuple-element.12.panel_ref, f32[4,2,8,128]{3,2,1,0:T(8,128)S(1)} %get-tuple-element.13.trail_ref, f32[1,64]{1,0:T(1,128)S(1)} %bitcast.5, ...), custom_call_target="tpu_custom_call" | custom-call | tf_op jit(solution)/shard_map/pallas_call | solution.py:362
Async XLA Ops:
  2.4 0.7 %copy-start = (f32[64]{0:T(128)S(1)}, f32[64]{0:T(128)}, u32[]{:S(2)}) copy-start(f32[64]{0:T(128)} %param.5) | copy-start | bytes 772

commit v4 on v3

--- a/solution.py
+++ b/solution.py
@@ -308,7 +308,7 @@
 def slab_kernel(
     n_row, n_col, block_rows,
     numbers, position, panel_ref, trail_ref, scales, one_ref, two_ref, second_ref, table_ref, rows_ref,
-    out_ref, keep_one, keep_two, chosen_ref,
+    out_ref, chosen_ref,
 ):
     signal = numbers[0]
     jitter = numbers[1]
@@ -323,31 +323,36 @@
 
     chunk = rows_ref.shape[0] * block_rows
     points = unpack(rows_ref[...]).reshape(chunk, FEAT) * scale
-    kernel = gaussian(chosen_ref[...], points, signal)
-    shape = kernel.shape
     group = BLK * n_col
-    col = lax.broadcasted_iota(jnp.int32, (shape[0], 1), 0)
-    extra = col - 2 * PANEL
-    owned = 2 * PANEL + extra // BLK * group + column * BLK + extra % BLK
-    col = jnp.where(extra >= 0, owned, col)
-    place = pl.program_id(0) * chunk + lax.broadcasted_iota(jnp.int32, (1, chunk), 1)
-    row = (place // block_rows * n_row + process_row) * block_rows + place % block_rows
-    kernel = kernel + jnp.where(col == row, jitter, 0.0)
-    first = full_dot(one_ref[...], kernel[:PANEL]).astype(jnp.bfloat16)
-    reduced = kernel[PANEL : 2 * PANEL] - plain_dot(second_ref[...], first)
-    second = full_dot(two_ref[...], reduced).astype(jnp.bfloat16)
-    trailing = kernel[2 * PANEL :] - (
-        plain_dot(table_ref[:, :PANEL], first) + plain_dot(table_ref[:, PANEL:], second)
+    blocks = PANEL // group
+    n_own = trail_ref.shape[0] * trail_ref.shape[1] * BLK
+
+    def place(shape, axis):
+        at = pl.program_id(0) * chunk + lax.broadcasted_iota(jnp.int32, shape, axis)
+        return (at // block_rows * n_row + process_row) * block_rows + at % block_rows
+
+    kernel = gaussian(points, chosen_ref[: 2 * PANEL], signal)
+    col = lax.broadcasted_iota(jnp.int32, (1, 2 * PANEL), 1)
+    kernel = kernel + jnp.where(place((chunk, 1), 0) == col, jitter, 0.0)
+    owned = gaussian(chosen_ref[2 * PANEL :], points, signal)
+    extra = lax.broadcasted_iota(jnp.int32, (n_own, 1), 0)
+    col = 2 * PANEL + extra // BLK * group + column * BLK + extra % BLK
+    owned = owned + jnp.where(place((1, chunk), 1) == col, jitter, 0.0)
+    across = ((1,), (1,))
+    first = full_dot(kernel[:, :PANEL], one_ref[...], across).astype(jnp.bfloat16)
+    reduced = kernel[:, PANEL:] - plain_dot(first, second_ref[...], across)
+    second = full_dot(reduced, two_ref[...], across).astype(jnp.bfloat16)
+    trailing = owned - (
+        plain_dot(table_ref[:, :PANEL], first, across) + plain_dot(table_ref[:, PANEL:], second, across)
     )
-    keep_one[...] = first.astype(jnp.float32)
-    keep_two[...] = second.astype(jnp.float32)
-    blocks = PANEL // group
-    for which, keep in enumerate((keep_one, keep_two)):
-        for t in range(blocks):
-            start = pl.multiple_of(t * group + column * BLK, BLK)
-            at = (which * blocks + t) * BLK
-            out_ref[at : at + BLK] = keep[pl.ds(start, BLK), :].reshape(BLK, 1, chunk)
-    out_ref[2 * blocks * BLK :] = trailing.reshape(trailing.shape[0], 1, chunk)
+    line = lax.broadcasted_iota(jnp.int32, (blocks * BLK, PANEL), 0)
+    wanted = line // BLK * group + column * BLK + line % BLK
+    chosen = (lax.broadcasted_iota(jnp.int32, line.shape, 1) == wanted).astype(jnp.float32)
+    chosen = chosen.astype(jnp.bfloat16)
+    half = blocks * BLK
+    out_ref[:half] = plain_dot(chosen, first, across).reshape(half, 1, chunk)
+    out_ref[half : 2 * half] = plain_dot(chosen, second, across).reshape(half, 1, chunk)
+    out_ref[2 * half :] = trailing.reshape(n_own, 1, chunk)
 
 
 def slab(numbers, position, factored, scales, n_row, n_col, block_rows):
@@ -367,8 +372,6 @@
         + [pl.BlockSpec((together, *rows.shape[1:]), lambda i: (i, 0, 0))],
         out_specs=pl.BlockSpec((n_out, 1, chunk), lambda i: (0, 0, i)),
         scratch_shapes=[
-            pltpu.VMEM((PANEL, chunk), jnp.float32),
-            pltpu.VMEM((PANEL, chunk), jnp.float32),
             pltpu.VMEM((2 * PANEL + n_own, FEAT), jnp.float32),
         ],
         compiler_params=pltpu.CompilerParams(vmem_limit_bytes=40 * 1024 * 1024),

time: 56.8 us -> 59.9 us (1.055)
  Pallas kernels: 53.6 us -> 56.6 us
    pallas_call x1, Pallas kernels: 11.6 us -> 14.6 us  [slab(): pl.pallas_call(functools.partial(slab_kernel, n_row, n_col, block_rows),...]
where the time goes in v4:
time: 59.9 us; the launch traced here: 59.7 us
  Pallas kernels  56.6 us (94%)
  local copies, waits for them, and re-layouts  1.58 us (3%)
  between operations  1.32 us (2%)
    pallas_call x1, Pallas kernels, exchange_and_factor(): pl.pallas_call(functools.partial(factor_kernel, n_row, n_col, n_panel, n_...  42 us
    pallas_call x1, Pallas kernels, slab(): pl.pallas_call(functools.partial(slab_kernel, n_row, n_col, block_rows),...  14.6 us
    unnamed x3, local copies, waits for them, and re-layouts  1.58 us

profile of v4, /device:TPU:24, one launch (start us, length us, event | category | flops | bytes accessed | tf_op | source)
XLA Modules:
  0.0 59.7 jit_solution(12371873232023080680)
XLA Ops:
  1.3 0.1 pad_maximum_fusion.numbers
  1.4 0.1 pad_add_fusion.position
  1.4 0.9 %copy.5.points = f32[256,64]{1,0:T(8,128)S(1)} copy(f32[256,64]{0,1:T(8,128)} %param.4) | data formatting | bytes 131072 | tf_op args[0]
  2.4 0.0 copy-start
  2.4 0.6 %copy-done = f32[64]{0:T(128)S(1)} copy-done((f32[64]{0:T(128)S(1)}, f32[64]{0:T(128)}, u32[]{:S(2)}) %copy-start) | copy-done | bytes 280
  3.0 42.0 %shard_map.46 = (f32[32,32,128]{2,1,0:T(8,128)S(1)}, f32[2,4,32,128]{3,2,1,0:T(8,128)S(1)}, f32[4,2,8,128]{3,2,1,0:T(8,128)S(1)}, f32[256,256]{1,0:T(8,128)S(1)}...) custom-call(f32[2]{0:T(128)S(1)} %pad_maximum_fusion.numbers, ...), custom_call_target="tpu_custom_call" | custom-call | tf_op jit(solution)/shard_map/pallas_call | solution.py:219
  45.1 14.6 %shard_map.47 = f32[192,1,2048]{2,1,0:T(1,128)} custom-call(f32[2]{0:T(128)S(1)} %pad_maximum_fusion.numbers, s32[2]{0:T(128)S(1)} %pad_add_fusion.position, f32[2,4,32,128]{3,2,1,0:T(8,128)S(1)} %get-tuple-element.12.panel_ref, f32[4,2,8,128]{3,2,1,0:T(8,128)S(1)} %get-tuple-element.13.trail_ref, f32[1,64]{1,0:T(1,128)S(1)} %bitcast.5, ...), custom_call_target="tpu_custom_call" | custom-call | tf_op jit(solution)/shard_map/pallas_call | solution.py:367
Async XLA Ops:
  2.4 0.7 %copy-start = (f32[64]{0:T(128)S(1)}, f32[64]{0:T(128)}, u32[]{:S(2)}) copy-start(f32[64]{0:T(128)} %param.5) | copy-start | bytes 772
